TPU v7x, 32 devices: a whole 2x2x4 slice. The times are simulated.
32 devices in a mesh: gx: 8 (over z, core), gy: 4 (over y, x).
Axes of the slice: x: 2, y: 2, z: 4, core: 2. Of those that a mesh axis runs over, the one named last changes fastest.
Arguments:
- density: float32 [32, 32, 128], P('gx', 'gy'), may hold values from 0.9 to 1.1
- velocity: float32 [3, 32, 32, 128], P(None, 'gx', 'gy'), may hold values from -0.625 to 0.625
- fluid_mask: int32 [32, 32, 128], P('gx', 'gy'), may hold values 0 or 1
- unit_of_column: int32 [32, 32], P('gx', 'gy'), may hold values from 0 to 31
- radius_base: float32 [256], P(('gx', 'gy')), may hold values from 0.5 to 2
Outputs:
- density_out: float32 [32, 32, 128], P('gx', 'gy')
- velocity_out: float32 [3, 32, 32, 128], P(None, 'gx', 'gy')
- radius_out: float32 [256], P(('gx', 'gy'))
All inputs are finite; a program needn't handle non-finite values. No bound on the sum of `fluid_mask` on one device may be relied on, other than what follows from the above.
Results may differ from a plain program's by a relative error of at most 0.0003.
Values sent between devices are 32-bit elements; how exact they have to be, the bound alone decides.
A program may use at most 64 MiB of HBM per device.

v0:
```python
import functools

import jax
import jax.numpy as jnp
from jax import lax
from jax.experimental import pallas as pl
from jax.experimental.pallas import tpu as pltpu
from jax.sharding import PartitionSpec as P

STEPS = 6

LATTICE = (
    (0, 0, 0),
    (1, 0, 0),
    (-1, 0, 0),
    (0, 1, 0),
    (0, -1, 0),
    (0, 0, 1),
    (0, 0, -1),
    (1, 1, 0),
    (-1, -1, 0),
    (1, -1, 0),
    (-1, 1, 0),
    (1, 0, 1),
    (-1, 0, -1),
    (1, 0, -1),
    (-1, 0, 1),
    (0, 1, 1),
    (0, -1, -1),
    (0, 1, -1),
    (0, -1, 1),
)
WEIGHTS = (1.0 / 3.0,) + (1.0 / 18.0,) * 6 + (1.0 / 36.0,) * 12
RELAX_RATE = 1.25
DRIVE_SCALE = 0.002
MESH = pl.DeviceIdType.MESH

X_DIRS = {s: [i for i, c in enumerate(LATTICE) if c[0] == s] for s in (1, -1)}
Y_DIRS = {s: [i for i, c in enumerate(LATTICE) if c[1] == s] for s in (1, -1)}
CORNERS = [i for i, c in enumerate(LATTICE) if c[0] and c[1]]


def reverse_of(direction):
    if direction == 0:
        return 0
    return direction + 1 if direction % 2 == 1 else direction - 1


def kernel(
    n_gx,
    n_gy,
    density_ref,
    velocity_ref,
    mask_ref,
    unit_ref,
    base_ref,
    density_out,
    velocity_out,
    radius_out,
    open_ref,
    links_ref,
    onehot_ref,
    row_ref,
    post_ref,
    rolled_ref,
    x_send,
    y_send,
    c_send,
    s_send,
    x_recv,
    y_recv,
    c_recv,
    s_recv,
    send_sem,
    recv_sem,
):
    size_x, size_y, size_z = density_ref.shape
    units_own = base_ref.shape[0]
    lanes = s_send.shape[-1]
    gx = lax.axis_index("gx")
    gy = lax.axis_index("gy")
    f32 = jnp.float32

    def inside(dx, dy):
        ok = None
        for pos, step, count in ((gx, dx, n_gx), (gy, dy, n_gy)):
            if step == 0:
                continue
            here = pos + step < count if step > 0 else pos + step >= 0
            ok = here if ok is None else jnp.logical_and(ok, here)
        return ok

    def messages(par):
        out = []
        for k, s in enumerate((1, -1)):
            out.append((s, 0, x_send.at[k], x_recv.at[par, k]))
        for k, s in enumerate((1, -1)):
            out.append((0, s, y_send.at[k], y_recv.at[par, k]))
        for k, i in enumerate(CORNERS):
            out.append((LATTICE[i][0], LATTICE[i][1], c_send.at[k], c_recv.at[par, k]))
        return [m + (n,) for n, m in enumerate(out)]

    def remote(par, dx, dy, src, dst, n):
        return pltpu.make_async_remote_copy(
            src_ref=src,
            dst_ref=dst,
            send_sem=send_sem.at[n],
            recv_sem=recv_sem.at[par, n],
            device_id=(gx + dx, gy + dy),
            device_id_type=MESH,
        )

    def row_copy(par, j, slot):
        return pltpu.make_async_remote_copy(
            src_ref=s_send,
            dst_ref=s_recv.at[par, slot],
            send_sem=send_sem.at[7 + j],
            recv_sem=recv_sem.at[par, 7 + j],
            device_id=(gx, lax.rem(gy + j, n_gy)),
            device_id_type=MESH,
        )

    def send_all(par):
        for j in range(1, n_gy):
            row_copy(par, j, gy).start()
        order = messages(par)
        for dx, dy, src, dst, n in order[4:] + order[:4]:
            pl.when(inside(dx, dy))(lambda: remote(par, dx, dy, src, dst, n).start())

    def wait_all(par):
        for j in range(1, n_gy):
            row_copy(par, j, lax.rem(gy - j + n_gy, n_gy)).wait()
        for dx, dy, src, dst, n in messages(par):
            pl.when(inside(-dx, -dy))(
                lambda: remote(par, dx, dy, src, dst, n).wait_recv()
            )
        for dx, dy, src, dst, n in messages(par):
            pl.when(inside(dx, dy))(lambda: remote(par, dx, dy, src, dst, n).wait_send())

    sublane = lax.broadcasted_iota(jnp.int32, (size_y, size_z), 0)
    lane = lax.broadcasted_iota(jnp.int32, (size_y, size_z), 1)

    def put(par, i, x, value):
        sx, sy, sz = LATTICE[i]
        if sz:
            value = pltpu.roll(value, sz % size_z, 1)
        if sy:
            value = pltpu.roll(value, sy % size_y, 0)
        rolled_ref[par, i, x] = value
        edge = size_x - 1 if sx > 0 else 0
        if sx and x == edge:
            side = 0 if sx > 0 else 1
            x_send[side, X_DIRS[sx].index(i)] = value
        if sy:
            side, row = (0, 0) if sy > 0 else (1, size_y - 1)
            line = value[row : row + 1, :]
            at = Y_DIRS[sy].index(i) * size_x + x
            y_send[side, at : at + 1, :] = line
            if sx and x == edge:
                c_send[CORNERS.index(i)] = line

    def pull(old, rx, i, x):
        sx, sy, sz = LATTICE[i]
        at = x - sx
        crossed = at < 0 or at >= size_x
        if crossed:
            value = x_recv[rx, 0 if sx > 0 else 1, X_DIRS[sx].index(i)]
        else:
            value = rolled_ref[old, i, at]
        if sy:
            side, row = (0, 0) if sy > 0 else (1, size_y - 1)
            if crossed:
                line = c_recv[rx, CORNERS.index(i)]
            else:
                slot = Y_DIRS[sy].index(i) * size_x + at
                line = y_recv[rx, side, slot : slot + 1, :]
            value = jnp.where(sublane == row, line, value)
        return value

    def total_rows(par):
        total = s_send[...]
        for j in range(n_gy):
            total = total + s_recv[par, j]
        return total

    def drive_tiles(radius_row):
        drive_row = (DRIVE_SCALE * radius_row) * radius_row
        return [
            jnp.sum(onehot_ref[x] * drive_row, axis=1, keepdims=True) for x in range(size_x)
        ]

    def relax(par, x, pops, rho, vel, drive):
        keep = 0.0 if pops is None else 1.0 - RELAX_RATE
        rate = 1.0 if pops is None else RELAX_RATE
        ux, uy, uz = vel
        speed = ux * ux + uy * uy + uz * uz
        rel = rate * rho
        level = rel - (1.5 * speed) * rel
        push = [(3.0 * rel) * u for u in vel]
        push[2] = push[2] + (3.0 * drive) * rho
        posts = [None] * 19
        rest = WEIGHTS[0] * level
        posts[0] = rest if pops is None else keep * pops[0] + rest
        for i in range(1, 19, 2):
            step = LATTICE[i]
            proj = None
            odd = None
            for comp in range(3):
                if step[comp] == 0:
                    continue
                if proj is None:
                    proj, odd = vel[comp], push[comp]
                elif step[comp] > 0:
                    proj, odd = proj + vel[comp], odd + push[comp]
                else:
                    proj, odd = proj - vel[comp], odd - push[comp]
            even = level + (4.5 * rel) * (proj * proj)
            for k, value in ((i, even + odd), (i + 1, even - odd)):
                value = WEIGHTS[i] * value
                posts[k] = value if pops is None else keep * pops[k] + value
        for i in range(19):
            post_ref[par, i, x] = posts[i]
            if i:
                put(par, i, x, posts[i])
        return speed

    def spread(x, speed):
        term = jnp.sum(links_ref[x] * speed, axis=1, keepdims=True)
        return onehot_ref[x] * term

    def gathered(old, rx, x, fl):
        pops = [post_ref[old, 0, x]]
        for i in range(1, 19):
            moved = pull(old, rx, i, x)
            pops.append(
                jnp.where(open_ref[i, x] > 0.0, moved, post_ref[old, reverse_of(i), x])
            )
        rho = pops[0]
        for i in range(1, 19):
            rho = rho + pops[i]
        momentum = []
        for comp in range(3):
            up = functools.reduce(
                lambda a, b: a + b, [pops[i] for i in range(19) if LATTICE[i][comp] == 1]
            )
            down = functools.reduce(
                lambda a, b: a + b, [pops[i] for i in range(19) if LATTICE[i][comp] == -1]
            )
            momentum.append(up - down)
        inverse = 1.0 / (rho + 1.0 - fl)
        return pops, rho, [m * inverse for m in momentum]

    def respond(par):
        total = total_rows(par)
        return row_ref[0:1, :] * (
            0.6
            + 0.8 * jnp.tanh(100.0 * total[0:1, :] / jnp.maximum(total[1:2, :], 1.0))
        )

    x_recv[...] = jnp.zeros_like(x_recv)
    y_recv[...] = jnp.zeros_like(y_recv)
    c_recv[...] = jnp.zeros_like(c_recv)
    s_recv[...] = jnp.zeros_like(s_recv)

    barrier = pltpu.get_barrier_semaphore()
    expected = jnp.int32(n_gy - 1)
    for j in range(1, n_gy):
        pl.semaphore_signal(
            barrier, inc=1, device_id=(gx, lax.rem(gy + j, n_gy)), device_id_type=MESH
        )
    for dx in (-1, 1):
        for dy in (-1, 0, 1):
            ok = inside(dx, dy)
            pl.when(ok)(
                lambda: pl.semaphore_signal(
                    barrier, inc=1, device_id=(gx + dx, gy + dy), device_id_type=MESH
                )
            )
            expected = expected + ok.astype(jnp.int32)

    shares = [mask_ref[x].astype(f32) for x in range(size_x)]
    for x in range(size_x):
        for i in range(1, 19):
            put(0, i, x, shares[x])
    wide = lax.broadcasted_iota(jnp.int32, (1, lanes), 1)
    own_row = jnp.zeros((1, lanes), f32)
    for j in range(units_own):
        own_row = jnp.where(wide == gy * units_own + j, base_ref[j], own_row)
    s_send[0:1, :] = own_row
    s_send[1:2, :] = jnp.zeros((1, lanes), f32)
    pl.semaphore_wait(barrier, expected)
    send_all(0)

    wide_y = lax.broadcasted_iota(jnp.int32, (size_y, lanes), 1)
    eye = lax.broadcasted_iota(jnp.int32, (size_y, size_y), 0) == lax.broadcasted_iota(
        jnp.int32, (size_y, size_y), 1
    )
    for x in range(size_x):
        names = jnp.broadcast_to(unit_ref[x : x + 1, :].astype(f32), (size_y, size_y))
        names = jnp.sum(jnp.where(eye, names, 0.0), axis=1, keepdims=True)
        onehot_ref[x] = jnp.where(wide_y.astype(f32) == names, 1.0, 0.0)

    wait_all(0)
    link_part = jnp.zeros((size_y, lanes), f32)
    for x in range(size_x):
        count = jnp.full((size_y, size_z), 18.0, f32)
        for i in range(1, 19):
            sz = LATTICE[i][2]
            value = pull(0, 0, i, x)
            if sz:
                value = jnp.where(lane == (0 if sz > 0 else size_z - 1), 0.0, value)
            value = value * shares[x]
            open_ref[i, x] = value
            count = count - value
        links_ref[x] = count * shares[x]
        link_part = link_part + spread(x, 1.0)
    row_ref[...] = total_rows(0)

    drives = drive_tiles(row_ref[0:1, :])
    part = jnp.zeros((size_y, lanes), f32)
    for x in range(size_x):
        rho = density_ref[x] * shares[x]
        vel = [velocity_ref[c, x] * shares[x] for c in range(3)]
        part = part + spread(x, relax(1, x, None, rho, vel, drives[x]))
    s_send[0:1, :] = jnp.sum(part, axis=0, keepdims=True)
    s_send[1:2, :] = jnp.sum(link_part, axis=0, keepdims=True)
    send_all(1)

    def step(r, carry):
        old = lax.rem(r, 2)
        new = 1 - old
        wait_all(old)
        drives = drive_tiles(respond(old))
        part = jnp.zeros((size_y, lanes), f32)
        for x in range(size_x):
            fl = mask_ref[x].astype(f32)
            pops, rho, vel = gathered(old, old, x, fl)
            part = part + spread(x, relax(new, x, pops, rho, vel, drives[x]))
        s_send[0:1, :] = jnp.sum(part, axis=0, keepdims=True)
        send_all(new)
        return carry

    lax.fori_loop(1, STEPS, step, 0)

    last = STEPS % 2
    wait_all(last)
    radius = respond(last)
    radius = pltpu.roll(
        jnp.broadcast_to(radius, (8, lanes)), lax.rem(lanes - gy * units_own, lanes), 1
    )
    radius_out[...] = radius[0:1, 0:units_own]
    for x in range(size_x):
        fl = mask_ref[x].astype(f32)
        pops, rho, vel = gathered(last, last, x, fl)
        density_out[x] = rho
        for comp in range(3):
            velocity_out[comp, x] = vel[comp]


def per_device(n_gx, n_gy, density, velocity, fluid_mask, unit_of_column, radius_base):
    size_x, size_y, size_z = density.shape
    units_own = radius_base.shape[0]
    lanes = -(-units_own * n_gy // 128) * 128
    f32 = jnp.float32
    tile = (size_x, size_y, size_z)
    copies = 7 + n_gy + 1
    vmem = pl.BlockSpec(memory_space=pltpu.VMEM)
    smem = pl.BlockSpec(memory_space=pltpu.SMEM)
    rho, vel, radius = pl.pallas_call(
        functools.partial(kernel, n_gx, n_gy),
        out_shape=(
            jax.ShapeDtypeStruct(density.shape, f32),
            jax.ShapeDtypeStruct(velocity.shape, f32),
            jax.ShapeDtypeStruct((1, units_own), f32),
        ),
        in_specs=[vmem, vmem, vmem, vmem, smem],
        out_specs=(vmem, vmem, vmem),
        scratch_shapes=[
            pltpu.VMEM((19,) + tile, f32),
            pltpu.VMEM(tile, f32),
            pltpu.VMEM((size_x, size_y, lanes), f32),
            pltpu.VMEM((2, lanes), f32),
            pltpu.VMEM((2, 19) + tile, f32),
            pltpu.VMEM((2, 19) + tile, f32),
            pltpu.VMEM((2, 5, size_y, size_z), f32),
            pltpu.VMEM((2, 5 * size_x, size_z), f32),
            pltpu.VMEM((4, 1, size_z), f32),
            pltpu.VMEM((2, lanes), f32),
            pltpu.VMEM((2, 2, 5, size_y, size_z), f32),
            pltpu.VMEM((2, 2, 5 * size_x, size_z), f32),
            pltpu.VMEM((2, 4, 1, size_z), f32),
            pltpu.VMEM((2, n_gy, 2, lanes), f32),
            pltpu.SemaphoreType.DMA((copies,)),
            pltpu.SemaphoreType.DMA((2, copies)),
        ],
        compiler_params=pltpu.CompilerParams(collective_id=0, has_side_effects=True),
    )(density, velocity, fluid_mask, unit_of_column, radius_base)
    return rho, vel, radius.reshape(units_own)


def solution(mesh):
    return jax.shard_map(
        functools.partial(per_device, mesh.shape["gx"], mesh.shape["gy"]),
        mesh=mesh,
        in_specs=(
            P("gx", "gy", None),
            P(None, "gx", "gy", None),
            P("gx", "gy", None),
            P("gx", "gy"),
            P(("gx", "gy")),
        ),
        out_specs=(P("gx", "gy", None), P(None, "gx", "gy", None), P(("gx", "gy"))),
        check_vma=False,
    )
```

profile of v0, /device:TPU:0, one launch (start us, length us, event | category | flops | bytes accessed | tf_op | source)
XLA Modules:
  0.0 35.0 jit_solution(1874964300615673535)
XLA Ops:
  0.6 31.1 %shard_map.76 = (f32[4,8,128]{2,1,0:T(8,128)}, f32[3,4,8,128]{3,2,1,0:T(8,128)}, f32[1,8]{1,0:T(1,128)}) custom-call(f32[4,8,128]{2,1,0:T(8,128)} %density_ref.1, f32[3,4,8,128]{3,2,1,0:T(8,128)} %velocity_ref.1, s32[4,8,128]{2,1,0:T(8,128)} %mask_ref.1, s32[4,8]{1,0:T(4,128)} %unit_ref.1, f32[8]{0:T(128)} %base_ref.1), custom_call_target="tpu_custom_call" | custom-call | tf_op jit(solution)/shard_map/pallas_call | solution.py:369
  31.8 1.3 %copy.11 = f32[4,8,128]{2,1,0:T(8,128)} copy(f32[4,8,128]{2,1,0:T(8,128)} %get-tuple-element.12) | data formatting | bytes 32768
  33.1 0.0 copy-start
  33.1 1.4 %copy.12 = f32[3,4,8,128]{3,2,1,0:T(8,128)} copy(f32[3,4,8,128]{3,2,1,0:T(8,128)} %get-tuple-element.13) | data formatting | bytes 98304
  34.5 0.0 copy-done
  34.5 0.5 %copy.13 = f32[8]{0:T(128)} copy(f32[8]{0:T(128)S(1)} %bitcast.1) | data formatting | bytes 64
Async XLA Ops:
  33.1 1.4 %copy-start = (f32[1,8]{1,0:T(1,128)S(1)}, f32[1,8]{1,0:T(1,128)}, u32[]{:S(2)}) copy-start(f32[1,8]{1,0:T(1,128)} %get-tuple-element.8) | copy-start | bytes 100
where the time goes:
time: 35.3 us; the launch traced here: 35 us
  Pallas kernels  31.1 us (88%)
  local copies, waits for them, and re-layouts  3.26 us (9%)
  between operations  0.64 us (2%)
    pallas_call x1, Pallas kernels, per_device(): pl.pallas_call(functools.partial(kernel, n_gx, n_gy), out_shape=(jax.Shap...  31.1 us
    unnamed x5, local copies, waits for them, and re-layouts  3.26 us

commit v1 on v0

--- a/solution.py
+++ b/solution.py
@@ -93,18 +93,18 @@
     def messages(par):
         out = []
         for k, s in enumerate((1, -1)):
-            out.append((s, 0, x_send.at[k], x_recv.at[par, k]))
+            out.append((s, 0, x_send.at[par, k], x_recv.at[par, k]))
         for k, s in enumerate((1, -1)):
-            out.append((0, s, y_send.at[k], y_recv.at[par, k]))
+            out.append((0, s, y_send.at[par, k], y_recv.at[par, k]))
         for k, i in enumerate(CORNERS):
-            out.append((LATTICE[i][0], LATTICE[i][1], c_send.at[k], c_recv.at[par, k]))
+            out.append((LATTICE[i][0], LATTICE[i][1], c_send.at[par, k], c_recv.at[par, k]))
         return [m + (n,) for n, m in enumerate(out)]
 
     def remote(par, dx, dy, src, dst, n):
         return pltpu.make_async_remote_copy(
             src_ref=src,
             dst_ref=dst,
-            send_sem=send_sem.at[n],
+            send_sem=send_sem.at[par, n],
             recv_sem=recv_sem.at[par, n],
             device_id=(gx + dx, gy + dy),
             device_id_type=MESH,
@@ -112,9 +112,9 @@
 
     def row_copy(par, j, slot):
         return pltpu.make_async_remote_copy(
-            src_ref=s_send,
+            src_ref=s_send.at[par],
             dst_ref=s_recv.at[par, slot],
-            send_sem=send_sem.at[7 + j],
+            send_sem=send_sem.at[par, 7 + j],
             recv_sem=recv_sem.at[par, 7 + j],
             device_id=(gx, lax.rem(gy + j, n_gy)),
             device_id_type=MESH,
@@ -129,11 +129,15 @@
 
     def wait_all(par):
         for j in range(1, n_gy):
-            row_copy(par, j, lax.rem(gy - j + n_gy, n_gy)).wait()
+            row_copy(par, j, lax.rem(gy - j + n_gy, n_gy)).wait_recv()
         for dx, dy, src, dst, n in messages(par):
             pl.when(inside(-dx, -dy))(
                 lambda: remote(par, dx, dy, src, dst, n).wait_recv()
             )
+
+    def wait_sent(par):
+        for j in range(1, n_gy):
+            row_copy(par, j, gy).wait_send()
         for dx, dy, src, dst, n in messages(par):
             pl.when(inside(dx, dy))(lambda: remote(par, dx, dy, src, dst, n).wait_send())
 
@@ -150,14 +154,14 @@
         edge = size_x - 1 if sx > 0 else 0
         if sx and x == edge:
             side = 0 if sx > 0 else 1
-            x_send[side, X_DIRS[sx].index(i)] = value
+            x_send[par, side, X_DIRS[sx].index(i)] = value
         if sy:
             side, row = (0, 0) if sy > 0 else (1, size_y - 1)
             line = value[row : row + 1, :]
             at = Y_DIRS[sy].index(i) * size_x + x
-            y_send[side, at : at + 1, :] = line
+            y_send[par, side, at : at + 1, :] = line
             if sx and x == edge:
-                c_send[CORNERS.index(i)] = line
+                c_send[par, CORNERS.index(i)] = line
 
     def pull(old, rx, i, x):
         sx, sy, sz = LATTICE[i]
@@ -178,7 +182,7 @@
         return value
 
     def total_rows(par):
-        total = s_send[...]
+        total = s_send[par]
         for j in range(n_gy):
             total = total + s_recv[par, j]
         return total
@@ -286,8 +290,8 @@
     own_row = jnp.zeros((1, lanes), f32)
     for j in range(units_own):
         own_row = jnp.where(wide == gy * units_own + j, base_ref[j], own_row)
-    s_send[0:1, :] = own_row
-    s_send[1:2, :] = jnp.zeros((1, lanes), f32)
+    s_send[0, 0:1, :] = own_row
+    s_send[0, 1:2, :] = jnp.zeros((1, lanes), f32)
     pl.semaphore_wait(barrier, expected)
     send_all(0)
 
@@ -322,9 +326,12 @@
         rho = density_ref[x] * shares[x]
         vel = [velocity_ref[c, x] * shares[x] for c in range(3)]
         part = part + spread(x, relax(1, x, None, rho, vel, drives[x]))
-    s_send[0:1, :] = jnp.sum(part, axis=0, keepdims=True)
-    s_send[1:2, :] = jnp.sum(link_part, axis=0, keepdims=True)
+    s_send[1, 0:1, :] = jnp.sum(part, axis=0, keepdims=True)
+    link_row = jnp.sum(link_part, axis=0, keepdims=True)
+    s_send[1, 1:2, :] = link_row
     send_all(1)
+    wait_sent(0)
+    s_send[0, 1:2, :] = link_row
 
     def step(r, carry):
         old = lax.rem(r, 2)
@@ -336,14 +343,16 @@
             fl = mask_ref[x].astype(f32)
             pops, rho, vel = gathered(old, old, x, fl)
             part = part + spread(x, relax(new, x, pops, rho, vel, drives[x]))
-        s_send[0:1, :] = jnp.sum(part, axis=0, keepdims=True)
+        s_send[new, 0:1, :] = jnp.sum(part, axis=0, keepdims=True)
         send_all(new)
+        wait_sent(old)
         return carry
 
     lax.fori_loop(1, STEPS, step, 0)
 
     last = STEPS % 2
     wait_all(last)
+    wait_sent(last)
     radius = respond(last)
     radius = pltpu.roll(
         jnp.broadcast_to(radius, (8, lanes)), lax.rem(lanes - gy * units_own, lanes), 1
@@ -355,6 +364,12 @@
         density_out[x] = rho
         for comp in range(3):
             velocity_out[comp, x] = vel[comp]
+
+
+def hand_over(rho, vel, radius, rho_out, vel_out, radius_out):
+    rho_out[...] = rho[...]
+    vel_out[...] = vel[...]
+    radius_out[...] = radius[...]
 
 
 def per_device(n_gx, n_gy, density, velocity, fluid_mask, unit_of_column, radius_base):
@@ -382,19 +397,29 @@
             pltpu.VMEM((2, lanes), f32),
             pltpu.VMEM((2, 19) + tile, f32),
             pltpu.VMEM((2, 19) + tile, f32),
-            pltpu.VMEM((2, 5, size_y, size_z), f32),
-            pltpu.VMEM((2, 5 * size_x, size_z), f32),
-            pltpu.VMEM((4, 1, size_z), f32),
-            pltpu.VMEM((2, lanes), f32),
+            pltpu.VMEM((2, 2, 5, size_y, size_z), f32),
+            pltpu.VMEM((2, 2, 5 * size_x, size_z), f32),
+            pltpu.VMEM((2, 4, 1, size_z), f32),
+            pltpu.VMEM((2, 2, lanes), f32),
             pltpu.VMEM((2, 2, 5, size_y, size_z), f32),
             pltpu.VMEM((2, 2, 5 * size_x, size_z), f32),
             pltpu.VMEM((2, 4, 1, size_z), f32),
             pltpu.VMEM((2, n_gy, 2, lanes), f32),
-            pltpu.SemaphoreType.DMA((copies,)),
+            pltpu.SemaphoreType.DMA((2, copies)),
             pltpu.SemaphoreType.DMA((2, copies)),
         ],
         compiler_params=pltpu.CompilerParams(collective_id=0, has_side_effects=True),
     )(density, velocity, fluid_mask, unit_of_column, radius_base)
+    rho, vel, radius = pl.pallas_call(
+        hand_over,
+        out_shape=(
+            jax.ShapeDtypeStruct(density.shape, f32),
+            jax.ShapeDtypeStruct(velocity.shape, f32),
+            jax.ShapeDtypeStruct((1, units_own), f32),
+        ),
+        in_specs=[vmem, vmem, vmem],
+        out_specs=(vmem, vmem, vmem),
+    )(rho, vel, radius)
     return rho, vel, radius.reshape(units_own)
 
 

time: 35.3 us -> 33.5 us (0.949)
  local copies, waits for them, and re-layouts: 3.26 us -> 0 us
  Pallas kernels: 31.1 us -> 32.6 us
    unnamed x5 -> x0, local copies, waits for them, and re-layouts: 3.26 us -> none
    pallas_call x0 -> x1, Pallas kernels: none -> 1.43 us  [per_device(): pl.pallas_call(hand_over, out_shape=(jax.ShapeDtypeStruct(density.shape,...]
where the time goes in v1:
time: 33.5 us; the launch traced here: 33.2 us
  Pallas kernels  32.6 us (97%)
  between operations  0.64 us (2%)
    pallas_call x1, Pallas kernels, per_device(): pl.pallas_call(functools.partial(kernel, n_gx, n_gy), out_shape=(jax.Shap...  31.2 us
    pallas_call x1, Pallas kernels, per_device(): pl.pallas_call(hand_over, out_shape=(jax.ShapeDtypeStruct(density.shape,...  1.43 us

profile of v1, /device:TPU:0, one launch (start us, length us, event | category | flops | bytes accessed | tf_op | source)
XLA Modules:
  0.0 33.2 jit_solution(14485127015352889734)
XLA Ops:
  0.6 31.2 %shard_map.76 = (f32[4,8,128]{2,1,0:T(8,128)}, f32[3,4,8,128]{3,2,1,0:T(8,128)}, f32[1,8]{1,0:T(1,128)}) custom-call(f32[4,8,128]{2,1,0:T(8,128)} %density_ref.1, f32[3,4,8,128]{3,2,1,0:T(8,128)} %velocity_ref.1, s32[4,8,128]{2,1,0:T(8,128)} %mask_ref.1, s32[4,8]{1,0:T(4,128)} %unit_ref.1, f32[8]{0:T(128)} %base_ref.1), custom_call_target="tpu_custom_call" | custom-call | tf_op jit(solution)/shard_map/pallas_call | solution.py:384
  31.8 1.4 %shard_map.77 = (f32[4,8,128]{2,1,0:T(8,128)}, f32[3,4,8,128]{3,2,1,0:T(8,128)}, f32[1,8]{1,0:T(1,128)}) custom-call(f32[4,8,128]{2,1,0:T(8,128)} %get-tuple-element.9.rho, f32[3,4,8,128]{3,2,1,0:T(8,128)} %get-tuple-element.10.vel, f32[1,8]{1,0:T(1,128)} %get-tuple-element.11.radius), custom_call_target="tpu_custom_call" | custom-call | tf_op jit(solution)/shard_map/pallas_call | solution.py:413

commit v2 on v1

--- a/solution.py
+++ b/solution.py
@@ -121,10 +121,12 @@
         )
 
     def send_all(par):
+        order = messages(par)
+        for dx, dy, src, dst, n in order[2:]:
+            pl.when(inside(dx, dy))(lambda: remote(par, dx, dy, src, dst, n).start())
         for j in range(1, n_gy):
             row_copy(par, j, gy).start()
-        order = messages(par)
-        for dx, dy, src, dst, n in order[4:] + order[:4]:
+        for dx, dy, src, dst, n in order[:2]:
             pl.when(inside(dx, dy))(lambda: remote(par, dx, dy, src, dst, n).start())
 
     def wait_all(par):

time: 33.5 us -> 33.7 us (level)
  no operation moved by 1% of the time
where the time goes in v2:
time: 33.7 us; the launch traced here: 33.5 us
  Pallas kernels  32.9 us (98%)
  between operations  0.64 us (2%)
    pallas_call x1, Pallas kernels, per_device(): pl.pallas_call(functools.partial(kernel, n_gx, n_gy), out_shape=(jax.Shap...  31.4 us
    pallas_call x1, Pallas kernels, per_device(): pl.pallas_call(hand_over, out_shape=(jax.ShapeDtypeStruct(density.shape,...  1.43 us

profile of v2, /device:TPU:0, one launch (start us, length us, event | category | flops | bytes accessed | tf_op | source)
XLA Modules:
  0.0 33.5 jit_solution(13419992294659617617)
XLA Ops:
  0.6 31.4 %shard_map.76 = (f32[4,8,128]{2,1,0:T(8,128)}, f32[3,4,8,128]{3,2,1,0:T(8,128)}, f32[1,8]{1,0:T(1,128)}) custom-call(f32[4,8,128]{2,1,0:T(8,128)} %density_ref.1, f32[3,4,8,128]{3,2,1,0:T(8,128)} %velocity_ref.1, s32[4,8,128]{2,1,0:T(8,128)} %mask_ref.1, s32[4,8]{1,0:T(4,128)} %unit_ref.1, f32[8]{0:T(128)} %base_ref.1), custom_call_target="tpu_custom_call" | custom-call | tf_op jit(solution)/shard_map/pallas_call | solution.py:386
  32.1 1.4 %shard_map.77 = (f32[4,8,128]{2,1,0:T(8,128)}, f32[3,4,8,128]{3,2,1,0:T(8,128)}, f32[1,8]{1,0:T(1,128)}) custom-call(f32[4,8,128]{2,1,0:T(8,128)} %get-tuple-element.9.rho, f32[3,4,8,128]{3,2,1,0:T(8,128)} %get-tuple-element.10.vel, f32[1,8]{1,0:T(1,128)} %get-tuple-element.11.radius), custom_call_target="tpu_custom_call" | custom-call | tf_op jit(solution)/shard_map/pallas_call | solution.py:415
